TPU v7x, 32 devices: a whole 2x2x4 slice. The times are simulated.
32 devices in a mesh: dp: 16 (over z, y, core), feat: 2 (over x).
Axes of the slice: x: 2, y: 2, z: 4, core: 2. Of those that a mesh axis runs over, the one named last changes fastest.
Arguments:
- table: bfloat16 [2048, 3584], P('dp', 'feat'), may hold values from -64 to 64
- text: bfloat16 [2048, 3584], P('dp', 'feat'), may hold values from -64 to 64
- table_proj: bfloat16 [3584, 4096], P(None, 'feat'), may hold values from -1 to 1
- text_proj: bfloat16 [3584, 4096], P(None, 'feat'), may hold values from -1 to 1
Outputs:
- grad_table: float32 [2048, 3584], P('dp', 'feat')
- grad_text: float32 [2048, 3584], P('dp', 'feat')
- loss_mean: float32 [1], replicated
All inputs are finite; a program needn't handle non-finite values.
Results may differ from a plain program's by a relative error of at most 0.0044.
Values may be sent and summed in bfloat16 or wider, within the bound.
No kernel may reach another device: no remote copies, remote signals or barrier semaphores. Data moves between devices by JAX's collectives and lax.ppermute only.
A program may use at most 128 MiB of HBM per device.

v0:
```python
import jax
import jax.numpy as jnp
from jax import lax
from jax.sharding import Mesh
from jax.sharding import PartitionSpec as P

OFF_WEIGHT = 0.1
EPS = 1e-05
Z_CHIPS = 4
F32 = jnp.float32
BF16 = jnp.bfloat16


def dot(a, b, dims):
    return lax.dot_general(a, b, (dims, ((), ())), preferred_element_type=F32)


def shift(x, axis, step):
    size = lax.axis_size(axis)
    return lax.ppermute(x, axis, [(i, (i + step) % size) for i in range(size)])


def flip(x, axis, bit=1):
    size = lax.axis_size(axis)
    return lax.ppermute(x, axis, [(i, i ^ bit) for i in range(size)])


def cube_sum(x, *axes):
    for axis in axes:
        bit = 1
        while bit < lax.axis_size(axis):
            x = x + flip(x, axis, bit)
            bit *= 2
    return x


def own_block(x, index, count, axis):
    size = x.shape[axis] // count
    return lax.dynamic_slice_in_dim(x, index * size, size, axis)


def both_cores(x, axis=0):
    got = flip(x, "core")
    first = lax.axis_index("core") == 0
    return jnp.where(first, jnp.concatenate([x, got], axis), jnp.concatenate([got, x], axis))


def add_cores(x, axis=0):
    core = lax.axis_index("core")
    return own_block(x, core, 2, axis) + flip(own_block(x, 1 - core, 2, axis), "core")


def weight_blocks(proj):
    num_feat = lax.axis_size("feat")
    feat = lax.axis_index("feat")
    cols = own_block(proj, lax.axis_index("core"), 2, 1)
    return [own_block(cols, (feat - step) % num_feat, num_feat, 0) for step in range(num_feat)]


def swap_feat(x):
    return [shift(x, "feat", step) for step in range(1, lax.axis_size("feat"))]


def project(z, others, weights):
    for other, weight in zip(others, weights[1:]):
        z = z + dot(both_cores(other), weight, ((1,), (0,)))
    return z


def gather_step(x, axis, bit):
    return jnp.concatenate([x, flip(x, axis, bit)], 0)


def merge(x):
    while x.shape[0] > 1:
        x = x[: x.shape[0] // 2] + x[x.shape[0] // 2 :]
    return x[0]


def split_two(x):
    high = x.astype(BF16)
    return high, (x - high.astype(F32)).astype(BF16)


def center_rows(z):
    mean = jnp.mean(z, axis=0)
    centered = z - mean
    return centered, mean, jnp.sum(centered * centered, axis=0)


def normalization(rows, means, squares, pairs):
    center = merge(means) / means.shape[0]
    offsets = means - center
    spread = (merge(squares) + rows * merge(offsets * offsets)) / pairs
    return lax.rsqrt(spread + EPS), offsets


def normalize_plane(centered, blocks, inverse, offsets):
    rows = [centered] + [block.astype(F32) for block in blocks]
    return jnp.concatenate([(part + offset) * inverse for part, offset in zip(rows, offsets)], 0)


def members(count, width):
    chips = jnp.repeat(jnp.arange(count, dtype=jnp.int32), width)
    return (jnp.arange(count, dtype=jnp.int32)[:, None] == chips[None, :]).astype(BF16)


def gram_part(plane, inverse, column, offsets):
    scaled = (plane * inverse).astype(BF16)
    count = offsets.shape[0]
    shifts = dot(scaled, jnp.concatenate(split_two(offsets), 0), ((1,), (1,)))
    shifts = jnp.concatenate(split_two(shifts[:, :count] + shifts[:, count:]), 1)
    chips = members(count, column.shape[0] // count)
    return dot(scaled, column, ((1,), (1,))) + dot(shifts, jnp.concatenate([chips, chips], 0), ((1,), (0,)))


def gram_times(gram, column, inverse, offsets):
    count = offsets.shape[0]
    sums = dot(gram, members(count, column.shape[0] // count), ((1,), (1,)))
    moved = lax.dot_general(
        sums, offsets, (((1,), (0,)), ((), ())), precision=lax.Precision.HIGHEST, preferred_element_type=F32
    )
    return inverse * (dot(gram, column, ((1,), (0,))) + moved)


def at_end(end, inner):
    z = lax.axis_index("z")
    return jnp.where((z == 0) | (z == Z_CHIPS - 1), end, inner)


def send_own(own):
    return flip(own, "z"), lax.ppermute(own, "z", [(1, 2), (2, 1)])


def send_near(near, mid):
    return lax.ppermute(near, "z", [(1, 2), (2, 1)]), lax.ppermute(mid, "z", [(1, 0), (2, 3)])


def send_far(far_in):
    return lax.ppermute(far_in, "z", [(1, 0), (2, 3)])


def over_y(x):
    return [flip(x, "y", step) for step in range(1, lax.axis_size("y"))]


def add_feat(mine, others):
    for other in others:
        mine = mine + other.astype(F32)
    return both_cores(mine.astype(BF16))


def column_sums(partial, plane, own, normed):
    return jnp.stack(
        [
            jnp.sum(partial, axis=0) + jnp.sum(own, axis=0),
            jnp.sum(partial * plane, axis=0) + jnp.sum(own * normed, axis=0),
        ]
    )


def returned(partial, rows):
    cut = rows // 2
    steps = range(1, lax.axis_size("y"))
    return [
        [flip(partial[step * rows + at : step * rows + at + cut].astype(BF16), "y", step) for step in steps] for at in (0, cut)
    ]


def add_returned(partial, got, own):
    d = partial[: own.shape[0]] + own
    for parts in zip(*got):
        d = d + jnp.concatenate(parts, 0).astype(F32)
    return d


def backward(d, normed, inverse, means):
    return (inverse * (d - means[0] - normed * means[1])).astype(BF16)


def swap_parts(sent):
    num_feat = lax.axis_size("feat")
    return [shift(part, "feat", num_feat - step) for step, part in enumerate(sent, 1)]


def body(table, text, table_proj, text_proj):
    pairs = table.shape[0] * 2 * lax.axis_size("z") * lax.axis_size("y")
    features = table_proj.shape[1] * lax.axis_size("feat")
    table_weights = weight_blocks(table_proj)
    text_weights = weight_blocks(text_proj)

    others_table = swap_feat(table)
    z_table = dot(both_cores(table), table_weights[0], ((1,), (0,)))
    z_text = dot(both_cores(text), text_weights[0], ((1,), (0,)))
    others_text = swap_feat(text)
    z_table, z_text, others_table = lax.optimization_barrier((z_table, z_text, others_table))
    z_table = project(z_table, others_table, table_weights)
    z_table, others_text = lax.optimization_barrier((z_table, others_text))
    rows = z_table.shape[0]
    y_size = lax.axis_size("y")
    centered_table, mean_table, square_table = center_rows(z_table)
    sent_rows_table = centered_table.astype(BF16)
    near_table, mid_table = send_own(sent_rows_table)

    z_text = project(z_text, others_text, text_weights)
    z_text, near_table, mid_table = lax.optimization_barrier((z_text, near_table, mid_table))
    centered_text, mean_text, square_text = center_rows(z_text)
    sent_rows_text = centered_text.astype(BF16)
    cross = jnp.sum(centered_table * centered_text, axis=0)
    stats = jnp.stack([mean_table, square_table, mean_text, square_text, cross])[None]
    while stats.shape[0] < y_size:
        stats = gather_step(stats, "y", stats.shape[0])

    stats = gather_step(stats, "z", 1)
    plane = over_y(jnp.stack([sent_rows_table, sent_rows_text]))
    far_in_table, far_end_table, near_text, mid_text, stats = lax.optimization_barrier(
        (*send_near(near_table, mid_table), *send_own(sent_rows_text), stats)
    )
    stats = gather_step(stats, "z", 2)
    last_end_table, far_in_text, far_end_text, stats = lax.optimization_barrier(
        (send_far(far_in_table), *send_near(near_text, mid_text), stats)
    )
    last_end_text = send_far(far_in_text)

    inverse_table, offsets_table = normalization(rows, stats[:, 0], stats[:, 1], pairs)
    inverse_text, offsets_text = normalization(rows, stats[:, 2], stats[:, 3], pairs)
    diag = inverse_table * inverse_text * ((merge(stats[:, 4]) + rows * merge(offsets_table * offsets_text)) / pairs)
    diag_weight = (diag - 1.0).astype(BF16).astype(F32) - OFF_WEIGHT * diag
    plane_table = normalize_plane(centered_table, [block[0] for block in plane], inverse_table, offsets_table)
    plane_text = normalize_plane(centered_text, [block[1] for block in plane], inverse_text, offsets_text)
    normed_table, normed_text = plane_table[:rows], plane_text[:rows]
    own_d_table = normed_text.astype(BF16).astype(F32) * diag_weight
    own_d_text = normed_table.astype(BF16).astype(F32) * diag_weight
    scale = OFF_WEIGHT / pairs
    moved_table, moved_text = offsets_table[::y_size], offsets_text[::y_size]

    last_table, far_table = at_end(last_end_table, mid_table), at_end(far_end_table, far_in_table)
    column_table = jnp.concatenate([sent_rows_table, near_table, far_table, last_table], 0)
    gram_table = add_cores(gram_part(plane_table, inverse_table, column_table, moved_table))
    others_gram_table = swap_feat(gram_table.astype(BF16))

    last_text, far_text = at_end(last_end_text, mid_text), at_end(far_end_text, far_in_text)
    column_text = jnp.concatenate([sent_rows_text, near_text, far_text, last_text], 0)
    gram_text = add_cores(gram_part(plane_text, inverse_text, column_text, moved_text))
    gram_table = add_feat(gram_table, others_gram_table)
    others_gram_text = swap_feat(gram_text.astype(BF16))
    partial_text = scale * gram_times(gram_table, column_text, inverse_text, moved_text)
    sums_text = cube_sum(column_sums(partial_text, plane_text, own_d_text, normed_text), "y")
    got_text = returned(partial_text, rows)
    sums_text = cube_sum(sums_text, "z")
    got_text[0], sums_text, others_gram_text = lax.optimization_barrier((got_text[0], sums_text, others_gram_text))

    gram_text = add_feat(gram_text, others_gram_text)
    partial_table = scale * gram_times(gram_text, column_table, inverse_table, moved_table)
    sums_table = column_sums(partial_table, plane_table, own_d_table, normed_table)
    sums_table, got_text[1] = lax.optimization_barrier((sums_table, got_text[1]))
    sums_table = cube_sum(sums_table, "y")
    d_text = add_returned(partial_text, got_text, own_d_text)
    back_text = backward(d_text, normed_text, inverse_text, sums_text / pairs)
    sums_table, back_text = lax.optimization_barrier((sums_table, back_text))
    got_table = returned(partial_table, rows)
    parts_text = [dot(back_text, weight, ((1,), (1,))) for weight in text_weights[1:]]
    sums_table = sums_table + flip(sums_table, "z", 1)
    sums_table, parts_text, got_table[0] = lax.optimization_barrier((sums_table, parts_text, got_table[0]))
    sent_text = [add_cores(part).astype(BF16) for part in parts_text]
    sums_table = sums_table + flip(sums_table, "z", 2)
    own_text = dot(back_text, text_weights[0], ((1,), (1,)))
    sent_text, own_text, sums_table = lax.optimization_barrier((sent_text, own_text, sums_table))
    grads_text = [swap_parts([jnp.split(part, 2)[i] for part in sent_text]) for i in range(2)]
    sums_table, got_table[1], grads_text[0] = lax.optimization_barrier((sums_table, got_table[1], grads_text[0]))

    means_table = sums_table / pairs
    d_table = add_returned(partial_table, got_table, own_d_table)
    back_table = backward(d_table, normed_table, inverse_table, means_table)
    parts_table = [dot(back_table, weight, ((1,), (1,))) for weight in table_weights[1:]]
    sent_table = [add_cores(part).astype(BF16) for part in parts_table]
    own_table = dot(back_table, table_weights[0], ((1,), (1,)))
    own_table, sent_table, grads_text[1] = lax.optimization_barrier((own_table, sent_table, grads_text[1]))
    grads_table = swap_parts(sent_table)

    squares = means_table[1] - diag_weight * diag
    terms = (1.0 - diag) * (1.0 - diag) - OFF_WEIGHT * diag * diag + squares
    loss_part, own_table = lax.optimization_barrier((jnp.sum(terms).reshape(1), own_table))
    loss_total = cube_sum(loss_part, "core", "feat")
    grads_text = [jnp.concatenate(parts, 0) for parts in zip(*grads_text)]
    grad_text = add_cores(own_text) + sum(part.astype(F32) for part in grads_text)
    grad_table = add_cores(own_table) + sum(part.astype(F32) for part in grads_table)
    return grad_table, grad_text, loss_total / features


def solution(mesh):
    devices = mesh.devices
    split = Mesh(
        devices.reshape(Z_CHIPS, devices.shape[0] // (2 * Z_CHIPS), 2, devices.shape[1]),
        ("z", "y", "core", "feat"),
    )
    rows = ("z", "y", "core")
    placed = (P(rows, "feat"), P(rows, "feat"), P(None, "feat"), P(None, "feat"))
    return jax.shard_map(
        body,
        mesh=split,
        in_specs=placed,
        out_specs=(P(rows, "feat"), P(rows, "feat"), P()),
        check_vma=False,
    )
```

profile of v0, /device:TPU:0, one launch (start us, length us, event | category | flops | bytes accessed | tf_op | source)
XLA Modules:
  0.0 221.1 jit_solution(7007515215389971450)
XLA Ops:
  1.2 2.9 %collective-permute-start.2 = (bf16[128,1792]{1,0:T(8,128)(2,1)}, bf16[128,1792]{1,0:T(8,128)(2,1)S(1)}, u32[]{:S(2)}, u32[]{:S(2)}) collective-permute-start(bf16[128,1792]{1,0:T(8,128)(2,1)} %param.4), channel_id=1, source_target_pairs={{0,1},{1,0},{2,3},{3,2},{4,5},{5,4},{6,7},{7,6},{8,9},{9,8},{10,11... | collective-permute-start | bytes 1376264 | tf_op jit(solution)/shard_map/ppermute | solution.py:20
  4.1 4.6 %fusion.10 = f32[256,1024]{1,0:T(8,128)S(1)} fusion(bf16[3584,2048]{1,0:T(8,128)(2,1)} %param.7, s32[]{:T(128)S(6)} %select_n.109, s32[]{:T(128)S(6)} %select_n.111, bf16[128,1792]{1,0:T(8,128)(2,1)S(1)} %collective-permute-done.1, bf16[128,1792]{1,0:T(8,128)(2,1)} %param.5, pred[]{:T(512)S(6)} %eq.43), kind=kOutput, calls=%fused_computation.10 | convolution fusion | flops 943652864 | bytes 5636105 | tf_op jit(solution)/shard_map/dot_general | solution.py:15
  8.8 4.6 %fusion.14 = f32[256,1024]{1,0:T(8,128)S(1)} fusion(bf16[3584,2048]{1,0:T(8,128)(2,1)} %param.6, s32[]{:T(128)S(6)} %select_n.109, s32[]{:T(128)S(6)} %select_n.111, bf16[128,1792]{1,0:T(8,128)(2,1)} %collective-permute-done, bf16[128,1792]{1,0:T(8,128)(2,1)S(1)} %copy-done.26, pred[]{:T(512)S(6)} %eq.43), kind=kOutput, calls=%fused_computation.14 | convolution fusion | flops 943652864 | bytes 5636105 | tf_op jit(solution)/shard_map/dot_general | solution.py:15
  16.9 4.3 %fusion.6 = f32[256,1024]{1,0:T(8,128)S(1)} fusion(bf16[3584,2048]{1,0:T(8,128)(2,1)} %param.6, s32[]{:T(128)S(6)} %select_n.116, s32[]{:T(128)S(6)} %select_n.111, bf16[128,1792]{1,0:T(8,128)(2,1)S(1)} %collective-permute-done.3, bf16[128,1792]{1,0:T(8,128)(2,1)S(1)} %collective-permute-done.2, pred[]{:T(512)S(6)} %eq.43), kind=kOutput, calls=%fused_computation.6 | convolution fusion | flops 943652864 | bytes 5636105 | tf_op jit(solution)/shard_map/dot_general | solution.py:15
  21.4 7.0 %collective-permute-done.4 = bf16[128,1792]{1,0:T(8,128)(2,1)} collective-permute-done((bf16[128,1792]{1,0:T(8,128)(2,1)}, bf16[128,1792]{1,0:T(8,128)(2,1)}, u32[]{:S(2)}, u32[]{:S(2)}) %collective-permute-start.4) | collective-permute-done | bytes 458784 | tf_op jit(solution)/shard_map/ppermute | solution.py:20
  30.1 3.9 %collective-permute-start.6 = (bf16[256,1024]{1,0:T(8,128)(2,1)S(1)}, bf16[256,1024]{1,0:T(8,128)(2,1)}, u32[]{:S(2)}, u32[]{:S(2)}) collective-permute-start(bf16[256,1024]{1,0:T(8,128)(2,1)S(1)} %subtract_convert_fusion.1), channel_id=1, source_target_pairs={{0,8},{8,0},{16,24},{24,16},{1,9},{9,1},{17,25},{25,17},{2,10},{10... | collective-permute-start | bytes 1572872 | tf_op jit(solution)/shard_map/ppermute | solution.py:25
  34.0 4.6 %fusion.2 = f32[256,1024]{1,0:T(8,128)S(1)} fusion(bf16[3584,2048]{1,0:T(8,128)(2,1)} %param.7, s32[]{:T(128)S(6)} %select_n.116, s32[]{:T(128)S(6)} %select_n.111, bf16[128,1792]{1,0:T(8,128)(2,1)S(1)} %collective-permute-done.5, bf16[128,1792]{1,0:T(8,128)(2,1)} %collective-permute-done.4, pred[]{:T(512)S(6)} %eq.43), kind=kOutput, calls=%fused_computation.2 | convolution fusion | flops 943652864 | bytes 5636105 | tf_op jit(solution)/shard_map/dot_general | solution.py:15
  38.8 7.6 %collective-permute-done.6 = bf16[256,1024]{1,0:T(8,128)(2,1)} collective-permute-done((bf16[256,1024]{1,0:T(8,128)(2,1)S(1)}, bf16[256,1024]{1,0:T(8,128)(2,1)}, u32[]{:S(2)}, u32[]{:S(2)}) %collective-permute-start.6) | collective-permute-done | bytes 524320 | tf_op jit(solution)/shard_map/ppermute | solution.py:25
  47.6 3.5 %collective-permute-start.10 = (bf16[256,1024]{1,0:T(8,128)(2,1)S(1)}, bf16[256,1024]{1,0:T(8,128)(2,1)}, u32[]{:S(2)}, u32[]{:S(2)}) collective-permute-start(bf16[256,1024]{1,0:T(8,128)(2,1)S(1)} %get-tuple-element.109), channel_id=1, source_target_pairs={{0,8},{8,0},{16,24},{24,16},{1,9},{9,1},{17,25},{25,17},{2,10},{10... | collective-permute-start | bytes 1572872 | tf_op jit(solution)/shard_map/ppermute | solution.py:25
  57.8 5.5 %collective-permute-start.13 = (f32[2,5,1024]{2,1,0:T(8,128)S(1)}, f32[2,5,1024]{2,1,0:T(8,128)S(1)}, u32[]{:S(2)}, u32[]{:S(2)}) collective-permute-start(f32[2,5,1024]{2,1,0:T(8,128)S(1)} %pad_maximum_fusion.11), channel_id=1, source_target_pairs={{0,8},{8,0},{16,24},{24,16},{1,9},{9,1},{17,25},{25,17},{2,10},{10... | collective-permute-start | bytes 122888 | tf_op jit(solution)/shard_map/ppermute | solution.py:25
  63.4 11.6 %collective-permute-done.13 = f32[2,5,1024]{2,1,0:T(8,128)S(1)} collective-permute-done((f32[2,5,1024]{2,1,0:T(8,128)S(1)}, f32[2,5,1024]{2,1,0:T(8,128)S(1)}, u32[]{:S(2)}, u32[]{:S(2)}) %collective-permute-start.13) | collective-permute-done | bytes 40992 | tf_op jit(solution)/shard_map/ppermute | solution.py:25
  81.0 5.4 %collective-permute-start.17 = (f32[4,5,1024]{2,1,0:T(8,128)S(1)}, f32[4,5,1024]{2,1,0:T(8,128)S(1)}, u32[]{:S(2)}, u32[]{:S(2)}) collective-permute-start(f32[4,5,1024]{2,1,0:T(8,128)S(1)} %pad_maximum_fusion.10), channel_id=1, source_target_pairs={{0,16},{8,24},{16,0},{24,8},{1,17},{9,25},{17,1},{25,9},{2,18},{10... | collective-permute-start | bytes 245768 | tf_op jit(solution)/shard_map/ppermute | solution.py:25
  88.3 11.5 %collective-permute-done.17 = f32[4,5,1024]{2,1,0:T(8,128)S(1)} collective-permute-done((f32[4,5,1024]{2,1,0:T(8,128)S(1)}, f32[4,5,1024]{2,1,0:T(8,128)S(1)}, u32[]{:S(2)}, u32[]{:S(2)}) %collective-permute-start.17) | collective-permute-done | bytes 81952 | tf_op jit(solution)/shard_map/ppermute | solution.py:25
  99.8 3.8 %collective-permute-done.16 = bf16[256,1024]{1,0:T(8,128)(2,1)S(1)} collective-permute-done((bf16[256,1024]{1,0:T(8,128)(2,1)S(1)}, bf16[256,1024]{1,0:T(8,128)(2,1)S(1)}, u32[]{:S(2)}, u32[]{:S(2)}) %collective-permute-start.16) | collective-permute-done | bytes 524320 | tf_op jit(solution)/shard_map/ppermute | solution.py:136
  123.0 10.3 %collective-permute-done.22 = bf16[256,1024]{1,0:T(8,128)(2,1)S(1)} collective-permute-done((bf16[256,1024]{1,0:T(8,128)(2,1)S(1)}, bf16[256,1024]{1,0:T(8,128)(2,1)S(1)}, u32[]{:S(2)}, u32[]{:S(2)}) %collective-permute-start.22) | collective-permute-done | bytes 524320 | tf_op jit(solution)/shard_map/ppermute | solution.py:20
  137.7 3.9 %fusion.115 = (f32[1024]{0:T(1024)S(1)}, f32[1024]{0:T(1024)S(1)}, bf16[512,1024]{1,0:T(8,128)(2,1)S(1)}, f32[512,1024]{1,0:T(8,128)}) fusion(f32[256,1024]{1,0:T(8,128)S(1)} %get-tuple-element.114, f32[256,1024]{1,0:T(8,128)S(1)} %get-tuple-element.132, f32[512,1024]{1,0:T(8,128)S(1)} %fusion.127, bf16[256,1024]{1,0:T(8,128)(2,1)S(1)} %broadcast_select_fusion.2, ...), kind=kOutput, calls=%fused_computation.220 | convolution fusion | flops 1091041280 | bytes 10498049 | tf_op jit(solution)/shard_map/dot_general | solution.py:15
  149.8 3.0 %collective-permute-start.27 = (f32[2,1024]{1,0:T(2,128)S(1)}, f32[2,1024]{1,0:T(2,128)S(1)}, u32[]{:S(2)}, u32[]{:S(2)}) collective-permute-start(f32[2,1024]{1,0:T(2,128)S(1)} %fusion.137), channel_id=1, source_target_pairs={{0,16},{8,24},{16,0},{24,8},{1,17},{9,25},{17,1},{25,9},{2,18},{10... | collective-permute-start | bytes 24584 | tf_op jit(solution)/shard_map/ppermute | solution.py:25
  159.3 4.6 %fusion.114 = (f32[1024]{0:T(1024)S(1)}, f32[1024]{0:T(1024)S(1)}, bf16[512,1024]{1,0:T(8,128)(2,1)S(1)}, f32[512,1024]{1,0:T(8,128)}) fusion(f32[256,1024]{1,0:T(8,128)S(1)} %copy-done.7, f32[256,1024]{1,0:T(8,128)S(1)} %get-tuple-element.131, f32[512,1024]{1,0:T(8,128)S(1)} %fusion.128, bf16[256,1024]{1,0:T(8,128)(2,1)S(1)} %copy-done.16, ...), kind=kOutput, calls=%fused_computation.219 | convolution fusion | flops 1091041280 | bytes 10498049 | tf_op jit(solution)/shard_map/dot_general | solution.py:15
  169.7 4.2 %fusion = f32[256,1792]{1,0:T(8,128)S(1)} fusion(bf16[256,1024]{1,0:T(8,128)(2,1)S(1)} %fusion.25, bf16[3584,2048]{1,0:T(8,128)(2,1)} %param.7, s32[]{:T(128)S(6)} %select_n.116, s32[]{:T(128)S(6)} %select_n.111), kind=kOutput, calls=%fused_computation | convolution fusion | flops 939524096 | bytes 6029320 | tf_op jit(solution)/shard_map/dot_general | solution.py:15
  178.1 4.2 %fusion.8 = f32[256,1792]{1,0:T(8,128)S(1)} fusion(bf16[256,1024]{1,0:T(8,128)(2,1)S(1)} %fusion.25, bf16[3584,2048]{1,0:T(8,128)(2,1)} %param.7, s32[]{:T(128)S(6)} %select_n.109, s32[]{:T(128)S(6)} %select_n.111), kind=kOutput, calls=%fused_computation.8 | convolution fusion | flops 939524096 | bytes 6029320 | tf_op jit(solution)/shard_map/dot_general | solution.py:15
  185.4 5.8 %collective-permute-done.37 = bf16[64,1792]{1,0:T(8,128)(2,1)S(1)} collective-permute-done((bf16[64,1792]{1,0:T(8,128)(2,1)S(1)}, bf16[64,1792]{1,0:T(8,128)(2,1)S(1)}, u32[]{:S(2)}, u32[]{:S(2)}) %collective-permute-start.37) | collective-permute-done | bytes 229408 | tf_op jit(solution)/shard_map/ppermute | solution.py:20
  192.6 4.2 %fusion.4 = f32[256,1792]{1,0:T(8,128)S(1)} fusion(bf16[256,1024]{1,0:T(8,128)(2,1)S(1)} %fusion.20, bf16[3584,2048]{1,0:T(8,128)(2,1)} %param.6, s32[]{:T(128)S(6)} %select_n.116, s32[]{:T(128)S(6)} %select_n.111), kind=kOutput, calls=%fused_computation.4 | convolution fusion | flops 939524096 | bytes 6029320 | tf_op jit(solution)/shard_map/dot_general | solution.py:15
  199.4 4.2 %fusion.12 = f32[256,1792]{1,0:T(8,128)S(1)} fusion(bf16[256,1024]{1,0:T(8,128)(2,1)S(1)} %fusion.20, bf16[3584,2048]{1,0:T(8,128)(2,1)} %param.6, s32[]{:T(128)S(6)} %select_n.109, s32[]{:T(128)S(6)} %select_n.111), kind=kOutput, calls=%fused_computation.12 | convolution fusion | flops 939524096 | bytes 6029320 | tf_op jit(solution)/shard_map/dot_general | solution.py:15
  209.5 7.7 %collective-permute-start.44 = (f32[1]{0:T(128)}, f32[1]{0:T(128)}, u32[]{:S(2)}, u32[]{:S(2)}) collective-permute-start(f32[1]{0:T(128)} %add.455), channel_id=1, source_target_pairs={{0,1},{1,0},{2,3},{3,2},{4,5},{5,4},{6,7},{7,6},{8,9},{9,8},{10,11... | collective-permute-start | bytes 20 | tf_op jit(solution)/shard_map/ppermute | solution.py:25
  (224 shorter events, 83.4 us)
Async XLA Ops:
  1.2 13.9 %collective-permute-start.2 = (bf16[128,1792]{1,0:T(8,128)(2,1)}, bf16[128,1792]{1,0:T(8,128)(2,1)S(1)}, u32[]{:S(2)}, u32[]{:S(2)}) collective-permute-start(bf16[128,1792]{1,0:T(8,128)(2,1)} %param.4), channel_id=1, source_target_pairs={{0,1},{1,0},{2,3},{3,2},{4,5},{5,4},{6,7},{7,6},{8,9},{9,8},{10,11... | collective-permute-start | bytes 1376264 | tf_op jit(solution)/shard_map/ppermute | solution.py:20
  15.1 13.2 %collective-permute-start.4 = (bf16[128,1792]{1,0:T(8,128)(2,1)}, bf16[128,1792]{1,0:T(8,128)(2,1)}, u32[]{:S(2)}, u32[]{:S(2)}) collective-permute-start(bf16[128,1792]{1,0:T(8,128)(2,1)} %param.5), channel_id=1, source_target_pairs={{0,1},{1,0},{2,3},{3,2},{4,5},{5,4},{6,7},{7,6},{8,9},{9,8},{10,11... | collective-permute-start | bytes 1376264 | tf_op jit(solution)/shard_map/ppermute | solution.py:20
  28.6 10.2 %collective-permute-start.7 = (bf16[256,1024]{1,0:T(8,128)(2,1)S(1)}, bf16[256,1024]{1,0:T(8,128)(2,1)}, u32[]{:S(2)}, u32[]{:S(2)}) collective-permute-start(bf16[256,1024]{1,0:T(8,128)(2,1)S(1)} %subtract_convert_fusion.1), channel_id=1, source_target_pairs={{8,16},{16,8},{9,17},{17,9},{10,18},{18,10},{11,19},{19,11},{12,20... | collective-permute-start | bytes 1572872 | tf_op jit(solution)/shard_map/ppermute | solution.py:132
  30.1 16.3 %collective-permute-start.6 = (bf16[256,1024]{1,0:T(8,128)(2,1)S(1)}, bf16[256,1024]{1,0:T(8,128)(2,1)}, u32[]{:S(2)}, u32[]{:S(2)}) collective-permute-start(bf16[256,1024]{1,0:T(8,128)(2,1)S(1)} %subtract_convert_fusion.1), channel_id=1, source_target_pairs={{0,8},{8,0},{16,24},{24,16},{1,9},{9,1},{17,25},{25,17},{2,10},{10... | collective-permute-start | bytes 1572872 | tf_op jit(solution)/shard_map/ppermute | solution.py:25
  46.9 28.1 %collective-permute-start.11 = (bf16[256,1024]{1,0:T(8,128)(2,1)S(1)}, bf16[256,1024]{1,0:T(8,128)(2,1)S(1)}, u32[]{:S(2)}, u32[]{:S(2)}) collective-permute-start(bf16[256,1024]{1,0:T(8,128)(2,1)S(1)} %get-tuple-element.109), channel_id=1, source_target_pairs={{8,16},{16,8},{9,17},{17,9},{10,18},{18,10},{11,19},{19,11},{12,20... | collective-permute-start | bytes 1572872 | tf_op jit(solution)/shard_map/ppermute | solution.py:132
  47.6 27.4 %collective-permute-start.10 = (bf16[256,1024]{1,0:T(8,128)(2,1)S(1)}, bf16[256,1024]{1,0:T(8,128)(2,1)}, u32[]{:S(2)}, u32[]{:S(2)}) collective-permute-start(bf16[256,1024]{1,0:T(8,128)(2,1)S(1)} %get-tuple-element.109), channel_id=1, source_target_pairs={{0,8},{8,0},{16,24},{24,16},{1,9},{9,1},{17,25},{25,17},{2,10},{10... | collective-permute-start | bytes 1572872 | tf_op jit(solution)/shard_map/ppermute | solution.py:25
  51.0 23.9 %collective-permute-start.9 = (bf16[256,1024]{1,0:T(8,128)(2,1)}, bf16[256,1024]{1,0:T(8,128)(2,1)}, u32[]{:S(2)}, u32[]{:S(2)}) collective-permute-start(bf16[256,1024]{1,0:T(8,128)(2,1)} %collective-permute-done.7), channel_id=1, source_target_pairs={{8,0},{16,24},{9,1},{17,25},{10,2},{18,26},{11,3},{19,27},{12,4},{... | collective-permute-start | bytes 1572872 | tf_op jit(solution)/shard_map/ppermute | solution.py:136
  52.3 22.7 %collective-permute-start.8 = (bf16[256,1024]{1,0:T(8,128)(2,1)}, bf16[256,1024]{1,0:T(8,128)(2,1)}, u32[]{:S(2)}, u32[]{:S(2)}) collective-permute-start(bf16[256,1024]{1,0:T(8,128)(2,1)} %collective-permute-done.6), channel_id=1, source_target_pairs={{8,16},{16,8},{9,17},{17,9},{10,18},{18,10},{11,19},{19,11},{12,20... | collective-permute-start | bytes 1572872 | tf_op jit(solution)/shard_map/ppermute | solution.py:136
  57.8 17.1 %collective-permute-start.13 = (f32[2,5,1024]{2,1,0:T(8,128)S(1)}, f32[2,5,1024]{2,1,0:T(8,128)S(1)}, u32[]{:S(2)}, u32[]{:S(2)}) collective-permute-start(f32[2,5,1024]{2,1,0:T(8,128)S(1)} %pad_maximum_fusion.11), channel_id=1, source_target_pairs={{0,8},{8,0},{16,24},{24,16},{1,9},{9,1},{17,25},{25,17},{2,10},{10... | collective-permute-start | bytes 122888 | tf_op jit(solution)/shard_map/ppermute | solution.py:25
  75.0 24.8 %collective-permute-start.14 = (bf16[256,1024]{1,0:T(8,128)(2,1)}, bf16[256,1024]{1,0:T(8,128)(2,1)S(1)}, u32[]{:S(2)}, u32[]{:S(2)}) collective-permute-start(bf16[256,1024]{1,0:T(8,128)(2,1)} %collective-permute-done.8), channel_id=1, source_target_pairs={{8,0},{16,24},{9,1},{17,25},{10,2},{18,26},{11,3},{19,27},{12,4},{... | collective-permute-start | bytes 1572872 | tf_op jit(solution)/shard_map/ppermute | solution.py:140
  76.3 27.3 %collective-permute-start.16 = (bf16[256,1024]{1,0:T(8,128)(2,1)S(1)}, bf16[256,1024]{1,0:T(8,128)(2,1)S(1)}, u32[]{:S(2)}, u32[]{:S(2)}) collective-permute-start(bf16[256,1024]{1,0:T(8,128)(2,1)S(1)} %collective-permute-done.11), channel_id=1, source_target_pairs={{8,0},{16,24},{9,1},{17,25},{10,2},{18,26},{11,3},{19,27},{12,4},{... | collective-permute-start | bytes 1572872 | tf_op jit(solution)/shard_map/ppermute | solution.py:136
  77.6 26.0 %collective-permute-start.15 = (bf16[256,1024]{1,0:T(8,128)(2,1)}, bf16[256,1024]{1,0:T(8,128)(2,1)S(1)}, u32[]{:S(2)}, u32[]{:S(2)}) collective-permute-start(bf16[256,1024]{1,0:T(8,128)(2,1)} %collective-permute-done.10), channel_id=1, source_target_pairs={{8,16},{16,8},{9,17},{17,9},{10,18},{18,10},{11,19},{19,11},{12,20... | collective-permute-start | bytes 1572872 | tf_op jit(solution)/shard_map/ppermute | solution.py:136
  79.5 28.7 %collective-permute-start.18 = (bf16[2,256,1024]{2,1,0:T(8,128)(2,1)}, bf16[2,256,1024]{2,1,0:T(8,128)(2,1)}, u32[]{:S(2)}, u32[]{:S(2)}) collective-permute-start(bf16[2,256,1024]{2,1,0:T(8,128)(2,1)} %pad_maximum_fusion.4), channel_id=1, source_target_pairs={{0,4},{4,0},{1,5},{5,1},{2,6},{6,2},{3,7},{7,3},{8,12},{12,8},{9,1... | collective-permute-start | bytes 3145736 | tf_op jit(solution)/shard_map/ppermute | solution.py:25
  81.0 18.8 %collective-permute-start.17 = (f32[4,5,1024]{2,1,0:T(8,128)S(1)}, f32[4,5,1024]{2,1,0:T(8,128)S(1)}, u32[]{:S(2)}, u32[]{:S(2)}) collective-permute-start(f32[4,5,1024]{2,1,0:T(8,128)S(1)} %pad_maximum_fusion.10), channel_id=1, source_target_pairs={{0,16},{8,24},{16,0},{24,8},{1,17},{9,25},{17,1},{25,9},{2,18},{10... | collective-permute-start | bytes 245768 | tf_op jit(solution)/shard_map/ppermute | solution.py:25
  104.9 13.8 %collective-permute-start.19 = (bf16[256,1024]{1,0:T(8,128)(2,1)}, bf16[256,1024]{1,0:T(8,128)(2,1)S(1)}, u32[]{:S(2)}, u32[]{:S(2)}) collective-permute-start(bf16[256,1024]{1,0:T(8,128)(2,1)} %copy-done.19), channel_id=1, source_target_pairs={{8,0},{16,24},{9,1},{17,25},{10,2},{18,26},{11,3},{19,27},{12,4},{... | collective-permute-start | bytes 1572872 | tf_op jit(solution)/shard_map/ppermute | solution.py:140
  121.3 12.0 %collective-permute-start.22 = (bf16[256,1024]{1,0:T(8,128)(2,1)S(1)}, bf16[256,1024]{1,0:T(8,128)(2,1)S(1)}, u32[]{:S(2)}, u32[]{:S(2)}) collective-permute-start(bf16[256,1024]{1,0:T(8,128)(2,1)S(1)} %fusion.55), channel_id=1, source_target_pairs={{0,1},{1,0},{2,3},{3,2},{4,5},{5,4},{6,7},{7,6},{8,9},{9,8},{10,11... | collective-permute-start | bytes 1572872 | tf_op jit(solution)/shard_map/ppermute | solution.py:20
  122.9 10.7 %collective-permute-start.20 = (f32[256,1024]{1,0:T(8,128)S(1)}, f32[256,1024]{1,0:T(8,128)S(1)}, u32[]{:S(2)}, u32[]{:S(2)}) collective-permute-start(f32[256,1024]{1,0:T(8,128)S(1)} %constant_dynamic-slice_fusion.5), channel_id=1, source_target_pairs={{0,2},{2,0},{1,3},{3,1},{4,6},{6,4},{5,7},{7,5},{8,10},{10,8},{9,1... | collective-permute-start | bytes 3145736 | tf_op jit(solution)/shard_map/ppermute | solution.py:25
  133.8 20.7 %collective-permute-start.28 = (bf16[256,1024]{1,0:T(8,128)(2,1)S(1)}, bf16[256,1024]{1,0:T(8,128)(2,1)S(1)}, u32[]{:S(2)}, u32[]{:S(2)}) collective-permute-start(bf16[256,1024]{1,0:T(8,128)(2,1)S(1)} %fusion.54), channel_id=1, source_target_pairs={{0,1},{1,0},{2,3},{3,2},{4,5},{5,4},{6,7},{7,6},{8,9},{9,8},{10,11... | collective-permute-start | bytes 1572872 | tf_op jit(solution)/shard_map/ppermute | solution.py:20
  143.3 11.1 %collective-permute-start.24 = (bf16[128,1024]{1,0:T(8,128)(2,1)S(1)}, bf16[128,1024]{1,0:T(8,128)(2,1)S(1)}, u32[]{:S(2)}, u32[]{:S(2)}) collective-permute-start(bf16[128,1024]{1,0:T(8,128)(2,1)S(1)} %get-tuple-element.113), channel_id=1, source_target_pairs={{0,4},{4,0},{1,5},{5,1},{2,6},{6,2},{3,7},{7,3},{8,12},{12,8},{9,1... | collective-permute-start | bytes 786440 | tf_op jit(solution)/shard_map/ppermute | solution.py:25
  154.8 9.2 %collective-permute-start.30 = (bf16[128,1024]{1,0:T(8,128)(2,1)S(1)}, bf16[128,1024]{1,0:T(8,128)(2,1)S(1)}, u32[]{:S(2)}, u32[]{:S(2)}) collective-permute-start(bf16[128,1024]{1,0:T(8,128)(2,1)S(1)} %get-tuple-element.112), channel_id=1, source_target_pairs={{0,4},{4,0},{1,5},{5,1},{2,6},{6,2},{3,7},{7,3},{8,12},{12,8},{9,1... | collective-permute-start | bytes 786440 | tf_op jit(solution)/shard_map/ppermute | solution.py:25
  175.3 10.1 %collective-permute-start.36 = (bf16[128,1024]{1,0:T(8,128)(2,1)}, bf16[128,1024]{1,0:T(8,128)(2,1)S(1)}, u32[]{:S(2)}, u32[]{:S(2)}) collective-permute-start(bf16[128,1024]{1,0:T(8,128)(2,1)} %get-tuple-element.110), channel_id=1, source_target_pairs={{0,4},{4,0},{1,5},{5,1},{2,6},{6,2},{3,7},{7,3},{8,12},{12,8},{9,1... | collective-permute-start | bytes 786440 | tf_op jit(solution)/shard_map/ppermute | solution.py:25
  205.1 13.7 %collective-permute-start.40 = (f32[128,1792]{1,0:T(8,128)S(1)}, f32[128,1792]{1,0:T(8,128)S(1)}, u32[]{:S(2)}, u32[]{:S(2)}) collective-permute-start(f32[128,1792]{1,0:T(8,128)S(1)} %constant_dynamic-slice_fusion.1), channel_id=1, source_target_pairs={{0,2},{2,0},{1,3},{3,1},{4,6},{6,4},{5,7},{7,5},{8,10},{10,8},{9,1... | collective-permute-start | bytes 2752520 | tf_op jit(solution)/shard_map/ppermute | solution.py:25
  205.6 13.2 %collective-permute-start.41 = (bf16[128,1792]{1,0:T(8,128)(2,1)S(1)}, bf16[128,1792]{1,0:T(8,128)(2,1)S(1)}, u32[]{:S(2)}, u32[]{:S(2)}) collective-permute-start(bf16[128,1792]{1,0:T(8,128)(2,1)S(1)} %add_convert_fusion.2), channel_id=1, source_target_pairs={{0,1},{1,0},{2,3},{3,2},{4,5},{5,4},{6,7},{7,6},{8,9},{9,8},{10,11... | collective-permute-start | bytes 1376264 | tf_op jit(solution)/shard_map/ppermute | solution.py:20
  209.5 8.7 %collective-permute-start.44 = (f32[1]{0:T(128)}, f32[1]{0:T(128)}, u32[]{:S(2)}, u32[]{:S(2)}) collective-permute-start(f32[1]{0:T(128)} %add.455), channel_id=1, source_target_pairs={{0,1},{1,0},{2,3},{3,2},{4,5},{5,4},{6,7},{7,6},{8,9},{9,8},{10,11... | collective-permute-start | bytes 20 | tf_op jit(solution)/shard_map/ppermute | solution.py:25
  (48 other events, 273.1 us)
where the time goes:
time: 222 us; the launch traced here: 221 us
  waiting for transfers between devices  72.9 us (33%)
  starting transfers between devices  69.4 us (31%)
  matrix products  54.3 us (24%)
  other arithmetic  15.3 us (7%)
  between operations  4.7 us (2%)
  local copies, waits for them, and re-layouts  4.44 us (2%)
    dot_general x18, matrix products, dot(): return lax.dot_general(a, b, (dims, ((), ())), preferred_element_type=F32)  50.8 us
    ppermute x30, starting transfers between devices, flip(): return lax.ppermute(x, axis, [(i, i ^ bit) for i in range(size)])  47.4 us
    ppermute x30, waiting for transfers between devices, flip(): return lax.ppermute(x, axis, [(i, i ^ bit) for i in range(size)])  40.4 us
    ppermute x7, waiting for transfers between devices, shift(): return lax.ppermute(x, axis, [(i, (i + step) % size) for i in range(size)])  25.9 us
    ppermute x7, starting transfers between devices, shift(): return lax.ppermute(x, axis, [(i, (i + step) % size) for i in range(size)])  12.4 us
  transfers between devices with their start and end apart: 45, of which 20 were waited for; matrix products, arithmetic and copies ran while one was open for 29% of the time, Pallas kernels for 0%

commit v1 on v0

--- a/solution.py
+++ b/solution.py
@@ -190,19 +190,22 @@
     text_weights = weight_blocks(text_proj)
 
     others_table = swap_feat(table)
+    tail_weights = lax.optimization_barrier((table_weights, text_weights))
     z_table = dot(both_cores(table), table_weights[0], ((1,), (0,)))
     z_text = dot(both_cores(text), text_weights[0], ((1,), (0,)))
     others_text = swap_feat(text)
     z_table, z_text, others_table = lax.optimization_barrier((z_table, z_text, others_table))
     z_table = project(z_table, others_table, table_weights)
     z_table, others_text = lax.optimization_barrier((z_table, others_text))
+    front_weights = text_weights
+    table_weights, text_weights = tail_weights
     rows = z_table.shape[0]
     y_size = lax.axis_size("y")
     centered_table, mean_table, square_table = center_rows(z_table)
     sent_rows_table = centered_table.astype(BF16)
     near_table, mid_table = send_own(sent_rows_table)
 
-    z_text = project(z_text, others_text, text_weights)
+    z_text = project(z_text, others_text, front_weights)
     z_text, near_table, mid_table = lax.optimization_barrier((z_text, near_table, mid_table))
     centered_text, mean_text, square_text = center_rows(z_text)
     sent_rows_text = centered_text.astype(BF16)
@@ -245,44 +248,43 @@
     gram_table = add_feat(gram_table, others_gram_table)
     others_gram_text = swap_feat(gram_text.astype(BF16))
     partial_text = scale * gram_times(gram_table, column_text, inverse_text, moved_text)
-    sums_text = cube_sum(column_sums(partial_text, plane_text, own_d_text, normed_text), "y")
     got_text = returned(partial_text, rows)
-    sums_text = cube_sum(sums_text, "z")
-    got_text[0], sums_text, others_gram_text = lax.optimization_barrier((got_text[0], sums_text, others_gram_text))
+    sums_text = column_sums(partial_text, plane_text, own_d_text, normed_text)
+    sums_text, got_text[0] = lax.optimization_barrier((sums_text, got_text[0]))
 
     gram_text = add_feat(gram_text, others_gram_text)
     partial_table = scale * gram_times(gram_text, column_table, inverse_table, moved_table)
     sums_table = column_sums(partial_table, plane_table, own_d_table, normed_table)
-    sums_table, got_text[1] = lax.optimization_barrier((sums_table, got_text[1]))
-    sums_table = cube_sum(sums_table, "y")
+    got_table = returned(partial_table, rows)
+    sums = cube_sum(jnp.concatenate([sums_text, sums_table], 0), "y")
+    sums, got_text[1] = lax.optimization_barrier((sums, got_text[1]))
+    sums = sums + flip(sums, "z", 1)
+    sums, got_table[0] = lax.optimization_barrier((sums, got_table[0]))
+    sums = sums + flip(sums, "z", 2)
+    sums, got_table[1] = lax.optimization_barrier((sums, got_table[1]))
+
+    means_text, means_table = sums[:2] / pairs, sums[2:] / pairs
     d_text = add_returned(partial_text, got_text, own_d_text)
-    back_text = backward(d_text, normed_text, inverse_text, sums_text / pairs)
-    sums_table, back_text = lax.optimization_barrier((sums_table, back_text))
-    got_table = returned(partial_table, rows)
+    d_table = add_returned(partial_table, got_table, own_d_table)
+    back_text = backward(d_text, normed_text, inverse_text, means_text)
     parts_text = [dot(back_text, weight, ((1,), (1,))) for weight in text_weights[1:]]
-    sums_table = sums_table + flip(sums_table, "z", 1)
-    sums_table, parts_text, got_table[0] = lax.optimization_barrier((sums_table, parts_text, got_table[0]))
+    d_table, parts_text = lax.optimization_barrier((d_table, parts_text))
     sent_text = [add_cores(part).astype(BF16) for part in parts_text]
-    sums_table = sums_table + flip(sums_table, "z", 2)
-    own_text = dot(back_text, text_weights[0], ((1,), (1,)))
-    sent_text, own_text, sums_table = lax.optimization_barrier((sent_text, own_text, sums_table))
-    grads_text = [swap_parts([jnp.split(part, 2)[i] for part in sent_text]) for i in range(2)]
-    sums_table, got_table[1], grads_text[0] = lax.optimization_barrier((sums_table, got_table[1], grads_text[0]))
-
-    means_table = sums_table / pairs
-    d_table = add_returned(partial_table, got_table, own_d_table)
     back_table = backward(d_table, normed_table, inverse_table, means_table)
     parts_table = [dot(back_table, weight, ((1,), (1,))) for weight in table_weights[1:]]
+    sent_text, parts_table, back_text = lax.optimization_barrier((sent_text, parts_table, back_text))
+    grads_text = swap_parts(sent_text)
     sent_table = [add_cores(part).astype(BF16) for part in parts_table]
+    back_text, back_table, sent_table = lax.optimization_barrier((back_text, back_table, sent_table))
+    own_text = dot(back_text, text_weights[0], ((1,), (1,)))
+    sent_table, own_text, *grads_text = lax.optimization_barrier((sent_table, own_text, *grads_text))
+    grads_table = swap_parts(sent_table)
     own_table = dot(back_table, table_weights[0], ((1,), (1,)))
-    own_table, sent_table, grads_text[1] = lax.optimization_barrier((own_table, sent_table, grads_text[1]))
-    grads_table = swap_parts(sent_table)
 
     squares = means_table[1] - diag_weight * diag
     terms = (1.0 - diag) * (1.0 - diag) - OFF_WEIGHT * diag * diag + squares
     loss_part, own_table = lax.optimization_barrier((jnp.sum(terms).reshape(1), own_table))
     loss_total = cube_sum(loss_part, "core", "feat")
-    grads_text = [jnp.concatenate(parts, 0) for parts in zip(*grads_text)]
     grad_text = add_cores(own_text) + sum(part.astype(F32) for part in grads_text)
     grad_table = add_cores(own_table) + sum(part.astype(F32) for part in grads_table)
     return grad_table, grad_text, loss_total / features

time: 222 us -> 238 us (1.072)
  waiting for transfers between devices: 72.9 us -> 108 us
  local copies, waits for them, and re-layouts: 4.44 us -> 24.8 us
  matrix products: 54.3 us -> 34.5 us
  starting transfers between devices: 69.4 us -> 51.6 us
    ppermute x30 -> x27, waiting for transfers between devices: 40.4 us -> 61.3 us  [flip(): return lax.ppermute(x, axis, [(i, i ^ bit) for i in range(size)])]
    dot_general x18, matrix products: 50.8 us -> 31 us  [dot(): return lax.dot_general(a, b, (dims, ((), ())), preferred_element_type=F32)]
    dynamic_slice x6 -> x8, local copies, waits for them, and re-layouts: 0.43 us -> 19.3 us  [own_block(): return lax.dynamic_slice_in_dim(x, index * size, size, axis)]
    ppermute x7 -> x6, waiting for transfers between devices: 25.9 us -> 38.1 us  [shift(): return lax.ppermute(x, axis, [(i, (i + step) % size) for i in range(size)])]
    ppermute x30 -> x27, starting transfers between devices: 47.4 us -> 37 us  [flip(): return lax.ppermute(x, axis, [(i, i ^ bit) for i in range(size)])]
    ppermute x7 -> x6, starting transfers between devices: 12.4 us -> 5.12 us  [shift(): return lax.ppermute(x, axis, [(i, (i + step) % size) for i in range(size)])]
    unnamed x56 -> x62, local copies, waits for them, and re-layouts: 2.95 us -> 5.19 us
  transfers between devices with their start and end apart: 45 -> 41, of which waited for: 20 -> 19; matrix products, arithmetic and copies ran while one was open for 29% -> 26% of each run, Pallas kernels for 0% -> 0%
where the time goes in v1:
time: 238 us
  waiting for transfers between devices  108 us (45%)
  starting transfers between devices  51.6 us (22%)
  matrix products  34.5 us (14%)
  local copies, waits for them, and re-layouts  24.8 us (10%)
  other arithmetic  14.4 us (6%)
  between operations  4.67 us (2%)
    ppermute x27, waiting for transfers between devices, flip(): return lax.ppermute(x, axis, [(i, i ^ bit) for i in range(size)])  61.3 us
    ppermute x6, waiting for transfers between devices, shift(): return lax.ppermute(x, axis, [(i, (i + step) % size) for i in range(size)])  38.1 us
    ppermute x27, starting transfers between devices, flip(): return lax.ppermute(x, axis, [(i, i ^ bit) for i in range(size)])  37 us
    dot_general x18, matrix products, dot(): return lax.dot_general(a, b, (dims, ((), ())), preferred_element_type=F32)  31 us
    dynamic_slice x8, local copies, waits for them, and re-layouts, own_block(): return lax.dynamic_slice_in_dim(x, index * size, size, axis)  19.3 us
    unnamed x62, local copies, waits for them, and re-layouts  5.19 us
    ppermute x6, starting transfers between devices, shift(): return lax.ppermute(x, axis, [(i, (i + step) % size) for i in range(size)])  5.12 us
  transfers between devices with their start and end apart: 41, of which 19 were waited for; matrix products, arithmetic and copies ran while one was open for 26% of the time, Pallas kernels for 0%

profile of v1, /device:TPU:0, one launch (start us, length us, event | category | flops | bytes accessed | tf_op | source)
XLA Modules:
  0.0 237.7 jit_solution(2262549798552611006)
XLA Ops:
  3.9 10.7 %fusion.104 = (bf16[1792,1024]{1,0:T(8,128)(2,1)}, bf16[1792,1024]{1,0:T(8,128)(2,1)}) fusion(bf16[3584,2048]{1,0:T(8,128)(2,1)} %param.6, s32[]{:T(128)S(6)} %select_n.116, s32[]{:T(128)S(6)} %select_n.111, s32[]{:T(128)S(6)} %select_n.109), kind=kLoop, calls=%fused_computation.207 | loop fusion | bytes 14680076 | tf_op jit(solution)/shard_map/dynamic_slice | solution.py:39
  14.6 7.2 %fusion.105 = (bf16[1792,1024]{1,0:T(8,128)(2,1)}, bf16[1792,1024]{1,0:T(8,128)(2,1)}) fusion(bf16[3584,2048]{1,0:T(8,128)(2,1)S(1)} %copy-done.2, s32[]{:T(128)S(6)} %select_n.116, s32[]{:T(128)S(6)} %select_n.111, s32[]{:T(128)S(6)} %select_n.109), kind=kLoop, calls=%fused_computation.208 | loop fusion | bytes 14680076 | tf_op jit(solution)/shard_map/dynamic_slice | solution.py:39
  21.8 3.3 %fusion.10 = f32[256,1024]{1,0:T(8,128)S(1)} fusion(bf16[1792,1024]{1,0:T(8,128)(2,1)} %get-tuple-element.77, bf16[128,1792]{1,0:T(8,128)(2,1)S(1)} %collective-permute-done, bf16[128,1792]{1,0:T(8,128)(2,1)S(1)} %copy-done.28, pred[]{:T(512)S(6)} %eq.43), kind=kOutput, calls=%fused_computation.44 | convolution fusion | flops 943652864 | bytes 5636097 | tf_op jit(solution)/shard_map/dot_general | solution.py:15
  29.6 9.8 %collective-permute-done.4 = bf16[128,1792]{1,0:T(8,128)(2,1)S(1)} collective-permute-done((bf16[128,1792]{1,0:T(8,128)(2,1)S(1)}, bf16[128,1792]{1,0:T(8,128)(2,1)S(1)}, u32[]{:S(2)}, u32[]{:S(2)}) %collective-permute-start.4) | collective-permute-done | bytes 458784 | tf_op jit(solution)/shard_map/ppermute | solution.py:20
  40.3 4.4 %collective-permute-start.6 = (bf16[256,1024]{1,0:T(8,128)(2,1)S(1)}, bf16[256,1024]{1,0:T(8,128)(2,1)}, u32[]{:S(2)}, u32[]{:S(2)}) collective-permute-start(bf16[256,1024]{1,0:T(8,128)(2,1)S(1)} %subtract_convert_fusion.1), channel_id=1, source_target_pairs={{0,8},{8,0},{16,24},{24,16},{1,9},{9,1},{17,25},{25,17},{2,10},{10... | collective-permute-start | bytes 1572872 | tf_op jit(solution)/shard_map/ppermute | solution.py:25
  44.7 3.5 %fusion.28 = f32[256,1024]{1,0:T(8,128)S(1)} fusion(bf16[1792,1024]{1,0:T(8,128)(2,1)} %get-tuple-element.70, bf16[128,1792]{1,0:T(8,128)(2,1)} %collective-permute-done.5, bf16[128,1792]{1,0:T(8,128)(2,1)S(1)} %collective-permute-done.4, pred[]{:T(512)S(6)} %eq.43), kind=kOutput, calls=%fused_computation.65 | convolution fusion | flops 943652864 | bytes 5636097 | tf_op jit(solution)/shard_map/dot_general | solution.py:15
  49.2 8.0 %collective-permute-done.6 = bf16[256,1024]{1,0:T(8,128)(2,1)} collective-permute-done((bf16[256,1024]{1,0:T(8,128)(2,1)S(1)}, bf16[256,1024]{1,0:T(8,128)(2,1)}, u32[]{:S(2)}, u32[]{:S(2)}) %collective-permute-start.6) | collective-permute-done | bytes 524320 | tf_op jit(solution)/shard_map/ppermute | solution.py:25
  59.0 3.1 %collective-permute-start.10 = (bf16[256,1024]{1,0:T(8,128)(2,1)S(1)}, bf16[256,1024]{1,0:T(8,128)(2,1)}, u32[]{:S(2)}, u32[]{:S(2)}) collective-permute-start(bf16[256,1024]{1,0:T(8,128)(2,1)S(1)} %get-tuple-element.123), channel_id=1, source_target_pairs={{0,8},{8,0},{16,24},{24,16},{1,9},{9,1},{17,25},{25,17},{2,10},{10... | collective-permute-start | bytes 1572872 | tf_op jit(solution)/shard_map/ppermute | solution.py:25
  68.9 5.1 %collective-permute-start.13 = (f32[2,5,1024]{2,1,0:T(8,128)S(1)}, f32[2,5,1024]{2,1,0:T(8,128)S(1)}, u32[]{:S(2)}, u32[]{:S(2)}) collective-permute-start(f32[2,5,1024]{2,1,0:T(8,128)S(1)} %pad_maximum_fusion.11), channel_id=1, source_target_pairs={{0,8},{8,0},{16,24},{24,16},{1,9},{9,1},{17,25},{25,17},{2,10},{10... | collective-permute-start | bytes 122888 | tf_op jit(solution)/shard_map/ppermute | solution.py:25
  74.0 12.4 %collective-permute-done.13 = f32[2,5,1024]{2,1,0:T(8,128)S(1)} collective-permute-done((f32[2,5,1024]{2,1,0:T(8,128)S(1)}, f32[2,5,1024]{2,1,0:T(8,128)S(1)}, u32[]{:S(2)}, u32[]{:S(2)}) %collective-permute-start.13) | collective-permute-done | bytes 40992 | tf_op jit(solution)/shard_map/ppermute | solution.py:25
  92.5 5.4 %collective-permute-start.17 = (f32[4,5,1024]{2,1,0:T(8,128)S(1)}, f32[4,5,1024]{2,1,0:T(8,128)S(1)}, u32[]{:S(2)}, u32[]{:S(2)}) collective-permute-start(f32[4,5,1024]{2,1,0:T(8,128)S(1)} %pad_maximum_fusion.10), channel_id=1, source_target_pairs={{0,16},{8,24},{16,0},{24,8},{1,17},{9,25},{17,1},{25,9},{2,18},{10... | collective-permute-start | bytes 245768 | tf_op jit(solution)/shard_map/ppermute | solution.py:25
  99.8 11.9 %collective-permute-done.17 = f32[4,5,1024]{2,1,0:T(8,128)S(1)} collective-permute-done((f32[4,5,1024]{2,1,0:T(8,128)S(1)}, f32[4,5,1024]{2,1,0:T(8,128)S(1)}, u32[]{:S(2)}, u32[]{:S(2)}) %collective-permute-start.17) | collective-permute-done | bytes 81952 | tf_op jit(solution)/shard_map/ppermute | solution.py:25
  111.7 3.8 %collective-permute-done.16 = bf16[256,1024]{1,0:T(8,128)(2,1)S(1)} collective-permute-done((bf16[256,1024]{1,0:T(8,128)(2,1)}, bf16[256,1024]{1,0:T(8,128)(2,1)S(1)}, u32[]{:S(2)}, u32[]{:S(2)}) %collective-permute-start.16) | collective-permute-done | bytes 524320 | tf_op jit(solution)/shard_map/ppermute | solution.py:136
  126.5 4.5 %collective-permute-done.22 = bf16[256,1024]{1,0:T(8,128)(2,1)S(1)} collective-permute-done((bf16[256,1024]{1,0:T(8,128)(2,1)}, bf16[256,1024]{1,0:T(8,128)(2,1)S(1)}, u32[]{:S(2)}, u32[]{:S(2)}) %collective-permute-start.22) | collective-permute-done | bytes 524320 | tf_op jit(solution)/shard_map/ppermute | solution.py:140
  134.4 10.4 %collective-permute-done.20 = bf16[256,1024]{1,0:T(8,128)(2,1)S(1)} collective-permute-done((bf16[256,1024]{1,0:T(8,128)(2,1)S(1)}, bf16[256,1024]{1,0:T(8,128)(2,1)S(1)}, u32[]{:S(2)}, u32[]{:S(2)}) %collective-permute-start.20) | collective-permute-done | bytes 524320 | tf_op jit(solution)/shard_map/ppermute | solution.py:20
  149.2 10.4 %collective-permute-done.25 = bf16[256,1024]{1,0:T(8,128)(2,1)S(1)} collective-permute-done((bf16[256,1024]{1,0:T(8,128)(2,1)S(1)}, bf16[256,1024]{1,0:T(8,128)(2,1)S(1)}, u32[]{:S(2)}, u32[]{:S(2)}) %collective-permute-start.25) | collective-permute-done | bytes 524320 | tf_op jit(solution)/shard_map/ppermute | solution.py:20
  160.0 3.9 %fusion.98 = (f32[1024]{0:T(1024)S(1)}, f32[1024]{0:T(1024)S(1)}, bf16[512,1024]{1,0:T(8,128)(2,1)S(1)}, f32[512,1024]{1,0:T(8,128)}) fusion(f32[256,1024]{1,0:T(8,128)S(1)} %get-tuple-element.129, f32[256,1024]{1,0:T(8,128)S(1)} %get-tuple-element.145, f32[512,1024]{1,0:T(8,128)S(1)} %fusion.112, bf16[256,1024]{1,0:T(8,128)(2,1)S(1)} %broadcast_select_fusion, ...), kind=kOutput, calls=%fused_computation.204 | convolution fusion | flops 1091041280 | bytes 10498049 | tf_op jit(solution)/shard_map/dot_general | solution.py:15
  166.1 7.1 %collective-permute-done.23 = bf16[128,1024]{1,0:T(8,128)(2,1)S(1)} collective-permute-done((bf16[128,1024]{1,0:T(8,128)(2,1)S(1)}, bf16[128,1024]{1,0:T(8,128)(2,1)S(1)}, u32[]{:S(2)}, u32[]{:S(2)}) %collective-permute-start.23) | collective-permute-done | bytes 262176 | tf_op jit(solution)/shard_map/ppermute | solution.py:25
  175.3 4.0 %fusion.99 = (f32[1024]{0:T(1024)S(1)}, f32[1024]{0:T(1024)S(1)}, bf16[512,1024]{1,0:T(8,128)(2,1)S(1)}, f32[512,1024]{1,0:T(8,128)}) fusion(f32[256,1024]{1,0:T(8,128)S(1)} %get-tuple-element.128, f32[256,1024]{1,0:T(8,128)S(1)} %get-tuple-element.146, f32[512,1024]{1,0:T(8,128)S(1)} %fusion.113, bf16[256,1024]{1,0:T(8,128)(2,1)S(1)} %broadcast_select_fusion.2, ...), kind=kOutput, calls=%fused_computation.205 | convolution fusion | flops 1091041280 | bytes 10498049 | tf_op jit(solution)/shard_map/dot_general | solution.py:15
  183.3 5.7 %collective-permute-done.27 = f32[4,1024]{1,0:T(4,128)S(1)} collective-permute-done((f32[4,1024]{1,0:T(4,128)S(1)}, f32[4,1024]{1,0:T(4,128)S(1)}, u32[]{:S(2)}, u32[]{:S(2)}) %collective-permute-start.27) | collective-permute-done | bytes 16416 | tf_op jit(solution)/shard_map/ppermute | solution.py:25
  193.7 3.9 %collective-permute-done.31 = f32[4,1024]{1,0:T(4,128)S(1)} collective-permute-done((f32[4,1024]{1,0:T(4,128)S(1)}, f32[4,1024]{1,0:T(4,128)S(1)}, u32[]{:S(2)}, u32[]{:S(2)}) %collective-permute-start.31) | collective-permute-done | bytes 16416 | tf_op jit(solution)/shard_map/ppermute | solution.py:25
  205.0 3.3 %fusion.115 = f32[256,1792]{1,0:T(8,128)S(1)} fusion(bf16[256,1024]{1,0:T(8,128)(2,1)S(1)} %multiply_convert_fusion.2, bf16[1792,1024]{1,0:T(8,128)(2,1)} %get-tuple-element.73), kind=kOutput, calls=%fused_computation.218 | convolution fusion | flops 939524096 | bytes 6029312 | tf_op jit(solution)/shard_map/dot_general | solution.py:15
  214.7 7.5 %collective-permute-done.36 = bf16[128,1792]{1,0:T(8,128)(2,1)S(1)} collective-permute-done((bf16[128,1792]{1,0:T(8,128)(2,1)S(1)}, bf16[128,1792]{1,0:T(8,128)(2,1)S(1)}, u32[]{:S(2)}, u32[]{:S(2)}) %collective-permute-start.36) | collective-permute-done | bytes 458784 | tf_op jit(solution)/shard_map/ppermute | solution.py:20
  226.4 5.5 %collective-permute-start.40 = (f32[1]{0:T(128)}, f32[1]{0:T(128)}, u32[]{:S(2)}, u32[]{:S(2)}) collective-permute-start(f32[1]{0:T(128)} %add.443), channel_id=1, source_target_pairs={{0,1},{1,0},{2,3},{3,2},{4,5},{5,4},{6,7},{7,6},{8,9},{9,8},{10,11... | collective-permute-start | bytes 20 | tf_op jit(solution)/shard_map/ppermute | solution.py:25
  (219 shorter events, 78.2 us)
Async XLA Ops:
  0.6 21.2 %collective-permute-start = (bf16[128,1792]{1,0:T(8,128)(2,1)}, bf16[128,1792]{1,0:T(8,128)(2,1)S(1)}, u32[]{:S(2)}, u32[]{:S(2)}) collective-permute-start(bf16[128,1792]{1,0:T(8,128)(2,1)} %param.4), channel_id=1, source_target_pairs={{0,2},{2,0},{1,3},{3,1},{4,6},{6,4},{5,7},{7,5},{8,10},{10,8},{9,1... | collective-permute-start | bytes 1376264 | tf_op jit(solution)/shard_map/ppermute | solution.py:25
  1.1 25.2 %collective-permute-start.2 = (bf16[128,1792]{1,0:T(8,128)(2,1)}, bf16[128,1792]{1,0:T(8,128)(2,1)S(1)}, u32[]{:S(2)}, u32[]{:S(2)}) collective-permute-start(bf16[128,1792]{1,0:T(8,128)(2,1)} %param.4), channel_id=1, source_target_pairs={{0,1},{1,0},{2,3},{3,2},{4,5},{5,4},{6,7},{7,6},{8,9},{9,8},{10,11... | collective-permute-start | bytes 1376264 | tf_op jit(solution)/shard_map/ppermute | solution.py:20
  3.7 21.4 %collective-permute-start.1 = (bf16[128,1792]{1,0:T(8,128)(2,1)}, bf16[128,1792]{1,0:T(8,128)(2,1)S(1)}, u32[]{:S(2)}, u32[]{:S(2)}) collective-permute-start(bf16[128,1792]{1,0:T(8,128)(2,1)} %param.5), channel_id=1, source_target_pairs={{0,2},{2,0},{1,3},{3,1},{4,6},{6,4},{5,7},{7,5},{8,10},{10,8},{9,1... | collective-permute-start | bytes 1376264 | tf_op jit(solution)/shard_map/ppermute | solution.py:25
  26.5 12.9 %collective-permute-start.4 = (bf16[128,1792]{1,0:T(8,128)(2,1)S(1)}, bf16[128,1792]{1,0:T(8,128)(2,1)S(1)}, u32[]{:S(2)}, u32[]{:S(2)}) collective-permute-start(bf16[128,1792]{1,0:T(8,128)(2,1)S(1)} %copy-done.29), channel_id=1, source_target_pairs={{0,1},{1,0},{2,3},{3,2},{4,5},{5,4},{6,7},{7,6},{8,9},{9,8},{10,11... | collective-permute-start | bytes 1376264 | tf_op jit(solution)/shard_map/ppermute | solution.py:20
  40.3 16.8 %collective-permute-start.6 = (bf16[256,1024]{1,0:T(8,128)(2,1)S(1)}, bf16[256,1024]{1,0:T(8,128)(2,1)}, u32[]{:S(2)}, u32[]{:S(2)}) collective-permute-start(bf16[256,1024]{1,0:T(8,128)(2,1)S(1)} %subtract_convert_fusion.1), channel_id=1, source_target_pairs={{0,8},{8,0},{16,24},{24,16},{1,9},{9,1},{17,25},{25,17},{2,10},{10... | collective-permute-start | bytes 1572872 | tf_op jit(solution)/shard_map/ppermute | solution.py:25
  57.5 28.9 %collective-permute-start.11 = (bf16[256,1024]{1,0:T(8,128)(2,1)S(1)}, bf16[256,1024]{1,0:T(8,128)(2,1)}, u32[]{:S(2)}, u32[]{:S(2)}) collective-permute-start(bf16[256,1024]{1,0:T(8,128)(2,1)S(1)} %get-tuple-element.123), channel_id=1, source_target_pairs={{8,16},{16,8},{9,17},{17,9},{10,18},{18,10},{11,19},{19,11},{12,20... | collective-permute-start | bytes 1572872 | tf_op jit(solution)/shard_map/ppermute | solution.py:132
  59.0 27.5 %collective-permute-start.10 = (bf16[256,1024]{1,0:T(8,128)(2,1)S(1)}, bf16[256,1024]{1,0:T(8,128)(2,1)}, u32[]{:S(2)}, u32[]{:S(2)}) collective-permute-start(bf16[256,1024]{1,0:T(8,128)(2,1)S(1)} %get-tuple-element.123), channel_id=1, source_target_pairs={{0,8},{8,0},{16,24},{24,16},{1,9},{9,1},{17,25},{25,17},{2,10},{10... | collective-permute-start | bytes 1572872 | tf_op jit(solution)/shard_map/ppermute | solution.py:25
  62.1 24.3 %collective-permute-start.9 = (bf16[256,1024]{1,0:T(8,128)(2,1)S(1)}, bf16[256,1024]{1,0:T(8,128)(2,1)}, u32[]{:S(2)}, u32[]{:S(2)}) collective-permute-start(bf16[256,1024]{1,0:T(8,128)(2,1)S(1)} %copy-done.16), channel_id=1, source_target_pairs={{8,0},{16,24},{9,1},{17,25},{10,2},{18,26},{11,3},{19,27},{12,4},{... | collective-permute-start | bytes 1572872 | tf_op jit(solution)/shard_map/ppermute | solution.py:136
  63.4 23.0 %collective-permute-start.8 = (bf16[256,1024]{1,0:T(8,128)(2,1)}, bf16[256,1024]{1,0:T(8,128)(2,1)}, u32[]{:S(2)}, u32[]{:S(2)}) collective-permute-start(bf16[256,1024]{1,0:T(8,128)(2,1)} %collective-permute-done.6), channel_id=1, source_target_pairs={{8,16},{16,8},{9,17},{17,9},{10,18},{18,10},{11,19},{19,11},{12,20... | collective-permute-start | bytes 1572872 | tf_op jit(solution)/shard_map/ppermute | solution.py:136
  68.9 17.5 %collective-permute-start.13 = (f32[2,5,1024]{2,1,0:T(8,128)S(1)}, f32[2,5,1024]{2,1,0:T(8,128)S(1)}, u32[]{:S(2)}, u32[]{:S(2)}) collective-permute-start(f32[2,5,1024]{2,1,0:T(8,128)S(1)} %pad_maximum_fusion.11), channel_id=1, source_target_pairs={{0,8},{8,0},{16,24},{24,16},{1,9},{9,1},{17,25},{25,17},{2,10},{10... | collective-permute-start | bytes 122888 | tf_op jit(solution)/shard_map/ppermute | solution.py:25
  86.5 25.2 %collective-permute-start.14 = (bf16[256,1024]{1,0:T(8,128)(2,1)}, bf16[256,1024]{1,0:T(8,128)(2,1)S(1)}, u32[]{:S(2)}, u32[]{:S(2)}) collective-permute-start(bf16[256,1024]{1,0:T(8,128)(2,1)} %collective-permute-done.8), channel_id=1, source_target_pairs={{8,0},{16,24},{9,1},{17,25},{10,2},{18,26},{11,3},{19,27},{12,4},{... | collective-permute-start | bytes 1572872 | tf_op jit(solution)/shard_map/ppermute | solution.py:140
  87.8 27.7 %collective-permute-start.16 = (bf16[256,1024]{1,0:T(8,128)(2,1)}, bf16[256,1024]{1,0:T(8,128)(2,1)S(1)}, u32[]{:S(2)}, u32[]{:S(2)}) collective-permute-start(bf16[256,1024]{1,0:T(8,128)(2,1)} %collective-permute-done.11), channel_id=1, source_target_pairs={{8,0},{16,24},{9,1},{17,25},{10,2},{18,26},{11,3},{19,27},{12,4},{... | collective-permute-start | bytes 1572872 | tf_op jit(solution)/shard_map/ppermute | solution.py:136
  89.1 26.4 %collective-permute-start.15 = (bf16[256,1024]{1,0:T(8,128)(2,1)}, bf16[256,1024]{1,0:T(8,128)(2,1)S(1)}, u32[]{:S(2)}, u32[]{:S(2)}) collective-permute-start(bf16[256,1024]{1,0:T(8,128)(2,1)} %collective-permute-done.10), channel_id=1, source_target_pairs={{8,16},{16,8},{9,17},{17,9},{10,18},{18,10},{11,19},{19,11},{12,20... | collective-permute-start | bytes 1572872 | tf_op jit(solution)/shard_map/ppermute | solution.py:136
  91.0 28.4 %collective-permute-start.18 = (bf16[2,256,1024]{2,1,0:T(8,128)(2,1)}, bf16[2,256,1024]{2,1,0:T(8,128)(2,1)}, u32[]{:S(2)}, u32[]{:S(2)}) collective-permute-start(bf16[2,256,1024]{2,1,0:T(8,128)(2,1)} %pad_maximum_fusion.4), channel_id=1, source_target_pairs={{0,4},{4,0},{1,5},{5,1},{2,6},{6,2},{3,7},{7,3},{8,12},{12,8},{9,1... | collective-permute-start | bytes 3145736 | tf_op jit(solution)/shard_map/ppermute | solution.py:25
  92.5 19.2 %collective-permute-start.17 = (f32[4,5,1024]{2,1,0:T(8,128)S(1)}, f32[4,5,1024]{2,1,0:T(8,128)S(1)}, u32[]{:S(2)}, u32[]{:S(2)}) collective-permute-start(f32[4,5,1024]{2,1,0:T(8,128)S(1)} %pad_maximum_fusion.10), channel_id=1, source_target_pairs={{0,16},{8,24},{16,0},{24,8},{1,17},{9,25},{17,1},{25,9},{2,18},{10... | collective-permute-start | bytes 245768 | tf_op jit(solution)/shard_map/ppermute | solution.py:25
  116.8 14.2 %collective-permute-start.22 = (bf16[256,1024]{1,0:T(8,128)(2,1)}, bf16[256,1024]{1,0:T(8,128)(2,1)S(1)}, u32[]{:S(2)}, u32[]{:S(2)}) collective-permute-start(bf16[256,1024]{1,0:T(8,128)(2,1)} %copy-done.20), channel_id=1, source_target_pairs={{8,0},{16,24},{9,1},{17,25},{10,2},{18,26},{11,3},{19,27},{12,4},{... | collective-permute-start | bytes 1572872 | tf_op jit(solution)/shard_map/ppermute | solution.py:140
  145.3 14.4 %collective-permute-start.25 = (bf16[256,1024]{1,0:T(8,128)(2,1)S(1)}, bf16[256,1024]{1,0:T(8,128)(2,1)S(1)}, u32[]{:S(2)}, u32[]{:S(2)}) collective-permute-start(bf16[256,1024]{1,0:T(8,128)(2,1)S(1)} %fusion.39), channel_id=1, source_target_pairs={{0,1},{1,0},{2,3},{3,2},{4,5},{5,4},{6,7},{7,6},{8,9},{9,8},{10,11... | collective-permute-start | bytes 1572872 | tf_op jit(solution)/shard_map/ppermute | solution.py:20
  159.9 13.2 %collective-permute-start.26 = (bf16[256,1024]{1,0:T(8,128)(2,1)S(1)}, bf16[256,1024]{1,0:T(8,128)(2,1)S(1)}, u32[]{:S(2)}, u32[]{:S(2)}) collective-permute-start(bf16[256,1024]{1,0:T(8,128)(2,1)S(1)} %add_convert_fusion), channel_id=1, source_target_pairs={{0,2},{2,0},{1,3},{3,1},{4,6},{6,4},{5,7},{7,5},{8,10},{10,8},{9,1... | collective-permute-start | bytes 1572872 | tf_op jit(solution)/shard_map/ppermute | solution.py:25
  165.6 23.5 %collective-permute-start.28 = (bf16[128,1024]{1,0:T(8,128)(2,1)S(1)}, bf16[128,1024]{1,0:T(8,128)(2,1)S(1)}, u32[]{:S(2)}, u32[]{:S(2)}) collective-permute-start(bf16[128,1024]{1,0:T(8,128)(2,1)S(1)} %get-tuple-element.126), channel_id=1, source_target_pairs={{0,4},{4,0},{1,5},{5,1},{2,6},{6,2},{3,7},{7,3},{8,12},{12,8},{9,1... | collective-permute-start | bytes 786440 | tf_op jit(solution)/shard_map/ppermute | solution.py:25
  179.4 13.5 %collective-permute-start.30 = (bf16[128,1024]{1,0:T(8,128)(2,1)S(1)}, bf16[128,1024]{1,0:T(8,128)(2,1)S(1)}, u32[]{:S(2)}, u32[]{:S(2)}) collective-permute-start(bf16[128,1024]{1,0:T(8,128)(2,1)S(1)} %get-tuple-element.125), channel_id=1, source_target_pairs={{0,4},{4,0},{1,5},{5,1},{2,6},{6,2},{3,7},{7,3},{8,12},{12,8},{9,1... | collective-permute-start | bytes 786440 | tf_op jit(solution)/shard_map/ppermute | solution.py:25
  181.8 15.9 %collective-permute-start.32 = (bf16[128,1024]{1,0:T(8,128)(2,1)S(1)}, bf16[128,1024]{1,0:T(8,128)(2,1)S(1)}, u32[]{:S(2)}, u32[]{:S(2)}) collective-permute-start(bf16[128,1024]{1,0:T(8,128)(2,1)S(1)} %get-tuple-element.124), channel_id=1, source_target_pairs={{0,4},{4,0},{1,5},{5,1},{2,6},{6,2},{3,7},{7,3},{8,12},{12,8},{9,1... | collective-permute-start | bytes 786440 | tf_op jit(solution)/shard_map/ppermute | solution.py:25
  209.8 12.4 %collective-permute-start.36 = (bf16[128,1792]{1,0:T(8,128)(2,1)S(1)}, bf16[128,1792]{1,0:T(8,128)(2,1)S(1)}, u32[]{:S(2)}, u32[]{:S(2)}) collective-permute-start(bf16[128,1792]{1,0:T(8,128)(2,1)S(1)} %add_convert_fusion.3), channel_id=1, source_target_pairs={{0,1},{1,0},{2,3},{3,2},{4,5},{5,4},{6,7},{7,6},{8,9},{9,8},{10,11... | collective-permute-start | bytes 1376264 | tf_op jit(solution)/shard_map/ppermute | solution.py:20
  212.7 21.8 %collective-permute-start.35 = (f32[128,1792]{1,0:T(8,128)S(1)}, f32[128,1792]{1,0:T(8,128)S(1)}, u32[]{:S(2)}, u32[]{:S(2)}) collective-permute-start(f32[128,1792]{1,0:T(8,128)S(1)} %constant_dynamic-slice_fusion.1), channel_id=1, source_target_pairs={{0,2},{2,0},{1,3},{3,1},{4,6},{6,4},{5,7},{7,5},{8,10},{10,8},{9,1... | collective-permute-start | bytes 2752520 | tf_op jit(solution)/shard_map/ppermute | solution.py:25
  222.8 12.7 %collective-permute-start.38 = (f32[128,1792]{1,0:T(8,128)S(1)}, f32[128,1792]{1,0:T(8,128)S(1)}, u32[]{:S(2)}, u32[]{:S(2)}) collective-permute-start(f32[128,1792]{1,0:T(8,128)S(1)} %constant_dynamic-slice_fusion), channel_id=1, source_target_pairs={{0,2},{2,0},{1,3},{3,1},{4,6},{6,4},{5,7},{7,5},{8,10},{10,8},{9,1... | collective-permute-start | bytes 2752520 | tf_op jit(solution)/shard_map/ppermute | solution.py:25
  (47 other events, 320.3 us)
